TPU v7x, 32 devices: a whole 2x2x4 slice. The times are simulated.
32 devices in a mesh: groups: 2 (over y), rows: 16 (over z, x, core).
Axes of the slice: x: 2, y: 2, z: 4, core: 2. Of those that a mesh axis runs over, the one named last changes fastest.
Arguments:
- hidden: bfloat16 [2, 4096, 8192], P(None, ('groups', 'rows')), parts along dimension 1, may hold values from -6 to 6
- q_base: bfloat16 [2, 4096, 768], P(None, ('groups', 'rows')), parts along dimension 1, may hold values from -22 to 22
- kv_base: bfloat16 [2, 4096, 256], P(None, ('groups', 'rows')), parts along dimension 1, may hold values from -6 to 6
- cache: bfloat16 [4096, 64, 256], P(('groups', 'rows')), parts along dimension 0, may hold values from -6 to 6
- lengths: int32 [4096], P(('groups', 'rows')), parts along dimension 0, may hold values from 2 to 64
- tenant: int32 [4096], P(('groups', 'rows')), parts along dimension 0, may hold values from 0 to 15, as said below
- slot_of_tenant: int32 [32], P('groups'), parts along dimension 0, may hold values from 0 to 15, each once
- bank_down: bfloat16 [32, 8192, 128], P(('groups', 'rows')), parts along dimension 0, may hold values from -0.0625 to 0.0625
- adapter_query_up_stack: bfloat16 [32, 64, 768], P(('groups', 'rows')), parts along dimension 0, may hold values from -0.75 to 0.75
- adapter_key_up_stack: bfloat16 [32, 64, 128], P(('groups', 'rows')), parts along dimension 0, may hold values from -0.75 to 0.75
Outputs:
- attended: bfloat16 [2, 4096, 768], P(None, ('groups', 'rows')), parts along dimension 1
There are 2 independent parts, one for each index of `groups`. A program takes and returns all parts, laid end to end along the dimension named above; each array names one. Nothing has to cross between parts.
Inputs may be any that keep to these rules, and one draw needn't show every extreme that they name: The rows of one device name one tenant at most 16 times; in every draw one tenant is named exactly 16 times by the rows of every device.
All inputs are finite; a program needn't handle non-finite values.
Results may differ from a plain program's by a relative error of at most 0.0077.
Values may be sent and summed in bfloat16 or wider, within the bound.
A program may use at most 128 MiB of HBM per device.

v0:
```python
import math

import jax
import jax.numpy as jnp
from jax import lax
from jax.sharding import PartitionSpec as P

NEG = -1e30


def attend(query, new_key, new_value, cache_keys, cache_values, length_block):
    steps_n, block_rows, width_q = query.shape
    head_dim = cache_keys.shape[2]
    head_count = width_q // head_dim
    positions_n = cache_keys.shape[1]
    score_scale = 1.0 / math.sqrt(head_dim)
    query_heads = query.reshape(steps_n, block_rows, head_count, head_dim)
    scores = (
        jnp.einsum("sbgh,bch->sbgc", query_heads, cache_keys, preferred_element_type=jnp.float32)
        * score_scale
    )
    in_cache = jnp.arange(positions_n, dtype=jnp.int32)[None, :] < length_block[:, None]
    scores = jnp.where(in_cache[None, :, None, :], scores, NEG)
    own_scores = (
        jnp.einsum("sbgh,tbh->sbgt", query_heads, new_key, preferred_element_type=jnp.float32)
        * score_scale
    )
    causal = jnp.arange(steps_n)[None, :] <= jnp.arange(steps_n)[:, None]
    own_scores = jnp.where(causal[:, None, None, :], own_scores, NEG)
    joined = jnp.concatenate([scores, own_scores], axis=-1)
    row_max = jnp.max(joined, axis=-1, keepdims=True)
    exponent = jnp.exp(joined - row_max)
    weights = (exponent / jnp.sum(exponent, axis=-1, keepdims=True)).astype(jnp.bfloat16)
    result = jnp.einsum(
        "sbgc,bch->sbgh",
        weights[..., :positions_n],
        cache_values,
        preferred_element_type=jnp.float32,
    )
    result = result + jnp.einsum(
        "sbgt,tbh->sbgh", weights[..., positions_n:], new_value, preferred_element_type=jnp.float32
    )
    return result.reshape(steps_n, block_rows, width_q).astype(jnp.bfloat16)


def local(
    hidden,
    q_base,
    kv_base,
    cache,
    lengths,
    tenant,
    slot_of_tenant,
    bank_down,
    adapter_query_up_stack,
    adapter_key_up_stack,
):
    peer_count = lax.axis_size("rows")
    steps_n, rows_here, model_width = hidden.shape
    capacity = max(2, (2 * rows_here + peer_count - 1) // peer_count)
    tenant_count = slot_of_tenant.shape[0]
    head_dim = cache.shape[2] // 2
    width_q = q_base.shape[2]
    rank_extent = adapter_query_up_stack.shape[1]
    tenant_ids = jnp.arange(tenant_count, dtype=jnp.int32)
    owner_dev = jnp.sum(
        jnp.where(tenant[:, None] == tenant_ids[None, :], slot_of_tenant[None, :], 0), axis=1
    )
    positions = jnp.arange(rows_here, dtype=jnp.int32)
    earlier = (tenant[:, None] == tenant[None, :]) & (positions[None, :] < positions[:, None])
    slot_column = owner_dev * capacity + jnp.sum(earlier.astype(jnp.int32), axis=1)
    placing = (
        slot_column[:, None] == jnp.arange(peer_count * capacity, dtype=jnp.int32)[None, :]
    ).astype(jnp.bfloat16)
    down_projected = bank_down[0]
    up_query = adapter_query_up_stack[0]
    up_key = adapter_key_up_stack[0]
    collected = []
    for step_index in range(steps_n):
        outgoing = jnp.einsum(
            "bc,bd->cd", placing, hidden[step_index], preferred_element_type=jnp.float32
        ).astype(jnp.bfloat16)
        outgoing = outgoing.reshape(peer_count, capacity, model_width)
        received = lax.all_to_all(outgoing, "rows", split_axis=0, concat_axis=0, tiled=True)
        flattened = received.reshape(-1, model_width)
        reduced_rank_input = jnp.dot(
            flattened, down_projected, preferred_element_type=jnp.float32
        ).astype(jnp.bfloat16)
        query_correction = jnp.dot(
            reduced_rank_input[:, :rank_extent], up_query, preferred_element_type=jnp.float32
        ).astype(jnp.bfloat16)
        key_correction = jnp.dot(
            reduced_rank_input[:, rank_extent:], up_key, preferred_element_type=jnp.float32
        ).astype(jnp.bfloat16)
        joined_delta = jnp.concatenate([query_correction, key_correction], axis=1)
        returned = lax.all_to_all(
            joined_delta.reshape(received.shape[0], received.shape[1], width_q + head_dim),
            "rows",
            split_axis=0,
            concat_axis=0,
            tiled=True,
        )
        returned = returned.reshape(peer_count * capacity, width_q + head_dim)
        collected.append(jnp.dot(placing, returned, preferred_element_type=jnp.float32))
    deltas = jnp.stack(collected)
    query = (q_base.astype(jnp.float32) + deltas[..., :width_q]).astype(jnp.bfloat16)
    new_key = (kv_base[..., :head_dim].astype(jnp.float32) + deltas[..., width_q:]).astype(
        jnp.bfloat16
    )
    new_value = kv_base[..., head_dim:]
    return attend(query, new_key, new_value, cache[..., :head_dim], cache[..., head_dim:], lengths)


def solution(mesh):
    return jax.shard_map(
        local,
        mesh=mesh,
        in_specs=(
            P(None, ("groups", "rows"), None),
            P(None, ("groups", "rows"), None),
            P(None, ("groups", "rows"), None),
            P(("groups", "rows"), None, None),
            P(("groups", "rows")),
            P(("groups", "rows")),
            P("groups"),
            P(("groups", "rows"), None, None),
            P(("groups", "rows"), None, None),
            P(("groups", "rows"), None, None),
        ),
        out_specs=P(None, ("groups", "rows"), None),
        check_vma=False,
    )
```

profile of v0, /device:TPU:17, one launch (start us, length us, event | category | flops | bytes accessed | tf_op | source)
XLA Modules:
  0.0 251.0 jit_solution(11182423909817049662)
XLA Ops:
  0.0 1.0 convert_reduce_fusion
  1.0 0.8 select_reduce_fusion
  1.8 4.9 %convolution_convert_fusion = bf16[256,8192]{1,0:T(8,128)(2,1)} fusion(bf16[2,128,8192]{2,1,0:T(8,128)(2,1)} %param.10, s32[128]{0:T(128)S(1)} %multiply_add_fusion), kind=kOutput, calls=%fused_computation | convolution fusion | flops 539000832 | bytes 6291968 | tf_op jit(solution)/shard_map/bc,bd->cd/dot_general | solution.py:80
  6.7 6.5 %all-to-all-start.2 = ((bf16[16,16,8192]{2,1,0:T(8,128)(2,1)}), bf16[16,16,8192]{2,1,0:T(8,128)(2,1)}, u32[]{:S(2)}, u32[]{:S(2)}) async-start(bf16[16,16,8192]{2,1,0:T(8,128)(2,1)} %bitcast.78), calls=%async_computation.2 | async-start | bytes 8388608 | tf_op jit(solution)/shard_map/all_to_all | solution.py:84
  13.2 4.9 %convolution_convert_fusion.1 = bf16[256,8192]{1,0:T(8,128)(2,1)} fusion(bf16[2,128,8192]{2,1,0:T(8,128)(2,1)} %param.10, s32[128]{0:T(128)S(1)} %multiply_add_fusion), kind=kOutput, calls=%fused_computation.1 | convolution fusion | flops 539000832 | bytes 6291968 | tf_op jit(solution)/shard_map/bc,bd->cd/dot_general | solution.py:80
  18.1 87.3 %all-to-all-done.2 = bf16[16,16,8192]{2,1,0:T(8,128)(2,1)} async-done(((bf16[16,16,8192]{2,1,0:T(8,128)(2,1)}), bf16[16,16,8192]{2,1,0:T(8,128)(2,1)}, u32[]{:S(2)}, u32[]{:S(2)}) %all-to-all-start.2) | async-done | bytes 4194336 | tf_op jit(solution)/shard_map/all_to_all | solution.py:84
  105.3 5.2 %all-to-all-start = ((bf16[16,16,8192]{2,1,0:T(8,128)(2,1)}), bf16[16,16,8192]{2,1,0:T(8,128)(2,1)}, u32[]{:S(2)}, u32[]{:S(2)}) async-start(bf16[16,16,8192]{2,1,0:T(8,128)(2,1)} %bitcast.77), calls=%async_computation | async-start | bytes 8388608 | tf_op jit(solution)/shard_map/all_to_all | solution.py:84
  110.6 3.7 %fusion.28 = bf16[256,128]{0,1:T(8,128)(2,1)S(1)} fusion(bf16[256,8192]{1,0:T(8,128)(2,1)} %bitcast.11, bf16[1,8192,128]{2,1,0:T(8,128)(2,1)S(1)} %copy-done), kind=kOutput, calls=%fused_computation.27 | convolution fusion | flops 536903680 | bytes 6356992 | tf_op jit(solution)/shard_map/dot_general | solution.py:86
  114.8 0.9 pad_maximum_fusion.1
  115.7 87.1 %all-to-all-done = bf16[16,16,8192]{2,1,0:T(8,128)(2,1)} async-done(((bf16[16,16,8192]{2,1,0:T(8,128)(2,1)}), bf16[16,16,8192]{2,1,0:T(8,128)(2,1)}, u32[]{:S(2)}, u32[]{:S(2)}) %all-to-all-start) | async-done | bytes 4194336 | tf_op jit(solution)/shard_map/all_to_all | solution.py:84
  202.7 5.2 %all-to-all-start.3 = ((bf16[16,16,896]{2,1,0:T(8,128)(2,1)}), bf16[16,16,896]{2,1,0:T(8,128)(2,1)S(1)}, u32[]{:S(2)}, u32[]{:S(2)}) async-start(bf16[16,16,896]{2,1,0:T(8,128)(2,1)} %bitcast.12), calls=%async_computation.3 | async-start | bytes 917504 | tf_op jit(solution)/shard_map/all_to_all | solution.py:96
  207.9 3.7 %fusion.25 = bf16[256,128]{0,1:T(8,128)(2,1)S(1)} fusion(bf16[256,8192]{1,0:T(8,128)(2,1)} %bitcast.2, bf16[1,8192,128]{2,1,0:T(8,128)(2,1)S(1)} %copy-done), kind=kOutput, calls=%fused_computation.26 | convolution fusion | flops 536903680 | bytes 6356992 | tf_op jit(solution)/shard_map/dot_general | solution.py:86
  212.1 0.8 pad_maximum_fusion
  212.9 6.8 %all-to-all-done.3 = bf16[16,16,896]{2,1,0:T(8,128)(2,1)S(1)} async-done(((bf16[16,16,896]{2,1,0:T(8,128)(2,1)}), bf16[16,16,896]{2,1,0:T(8,128)(2,1)S(1)}, u32[]{:S(2)}, u32[]{:S(2)}) %all-to-all-start.3) | async-done | bytes 458784 | tf_op jit(solution)/shard_map/all_to_all | solution.py:96
  219.7 5.3 %all-to-all-start.1 = ((bf16[16,16,896]{2,1,0:T(8,128)(2,1)}), bf16[16,16,896]{2,1,0:T(8,128)(2,1)S(1)}, u32[]{:S(2)}, u32[]{:S(2)}) async-start(bf16[16,16,896]{2,1,0:T(8,128)(2,1)} %bitcast.6), calls=%async_computation.1 | async-start | bytes 917504 | tf_op jit(solution)/shard_map/all_to_all | solution.py:96
  225.4 11.4 %all-to-all-done.1 = bf16[16,16,896]{2,1,0:T(8,128)(2,1)S(1)} async-done(((bf16[16,16,896]{2,1,0:T(8,128)(2,1)}), bf16[16,16,896]{2,1,0:T(8,128)(2,1)S(1)}, u32[]{:S(2)}, u32[]{:S(2)}) %all-to-all-start.1) | async-done | bytes 458784 | tf_op jit(solution)/shard_map/all_to_all | solution.py:96
  237.2 0.9 fusion.42
  238.0 1.1 fusion.34
  239.8 2.4 fusion.43
  243.1 3.3 %fusion.57 = (f32[2,128,6]{2,0,1:T(2,128)S(1)}, f32[2,128,6,64]{3,2,0,1:T(8,128)S(1)}) fusion(bf16[2,128,6,128]{3,2,0,1:T(8,128)(2,1)} %copy-done.1, bf16[128,64,256]{2,1,0:T(8,128)(2,1)} %param.13, pred[128,64]{1,0:T(8,128)(4,1)S(1)} %iota_compare_fusion.6), kind=kOutput, calls=%fused_computation.73 | convolution fusion | flops 25459200 | bytes 3028992 | tf_op jit(solution)/shard_map/sbgh,bch->sbgc/dot_general | solution.py:19
  246.4 1.1 fusion.37
  247.5 1.0 divide_convert_fusion
  248.6 0.7 fusion
  250.1 0.9 copy.92
  (32 shorter events, 4.0 us)
Async XLA Ops:
  0.0 110.6 %copy-start = (bf16[1,8192,128]{2,1,0:T(8,128)(2,1)S(1)}, bf16[1,8192,128]{2,1,0:T(8,128)(2,1)}, u32[]{:S(2)}) copy-start(bf16[1,8192,128]{2,1,0:T(8,128)(2,1)} %param.17) | copy-start | bytes 6291460
  6.7 98.7 %all-to-all-start.2 = ((bf16[16,16,8192]{2,1,0:T(8,128)(2,1)}), bf16[16,16,8192]{2,1,0:T(8,128)(2,1)}, u32[]{:S(2)}, u32[]{:S(2)}) async-start(bf16[16,16,8192]{2,1,0:T(8,128)(2,1)} %bitcast.78), calls=%async_computation.2 | async-start | bytes 8388608 | tf_op jit(solution)/shard_map/all_to_all | solution.py:84
  105.3 97.4 %all-to-all-start = ((bf16[16,16,8192]{2,1,0:T(8,128)(2,1)}), bf16[16,16,8192]{2,1,0:T(8,128)(2,1)}, u32[]{:S(2)}, u32[]{:S(2)}) async-start(bf16[16,16,8192]{2,1,0:T(8,128)(2,1)} %bitcast.77), calls=%async_computation | async-start | bytes 8388608 | tf_op jit(solution)/shard_map/all_to_all | solution.py:84
  110.5 3.8 %copy-start.4 = (bf16[1,64,128]{2,1,0:T(8,128)(2,1)S(1)}, bf16[1,64,128]{2,1,0:T(8,128)(2,1)}, u32[]{:S(2)}) copy-start(bf16[1,64,128]{2,1,0:T(8,128)(2,1)} %param.19) | copy-start | bytes 49156
  110.5 4.0 %copy-start.3 = (bf16[1,64,768]{2,1,0:T(8,128)(2,1)S(1)}, bf16[1,64,768]{2,1,0:T(8,128)(2,1)}, u32[]{:S(2)}) copy-start(bf16[1,64,768]{2,1,0:T(8,128)(2,1)} %param.18) | copy-start | bytes 294916
  202.7 17.0 %all-to-all-start.3 = ((bf16[16,16,896]{2,1,0:T(8,128)(2,1)}), bf16[16,16,896]{2,1,0:T(8,128)(2,1)S(1)}, u32[]{:S(2)}, u32[]{:S(2)}) async-start(bf16[16,16,896]{2,1,0:T(8,128)(2,1)} %bitcast.12), calls=%async_computation.3 | async-start | bytes 917504 | tf_op jit(solution)/shard_map/all_to_all | solution.py:96
  207.9 17.2 %copy-start.5 = (s32[128]{0:T(128)S(1)}, s32[128]{0:T(128)}, u32[]{:S(2)}) copy-start(s32[128]{0:T(128)} %param.14) | copy-start | bytes 1540
  219.7 17.2 %all-to-all-start.1 = ((bf16[16,16,896]{2,1,0:T(8,128)(2,1)}), bf16[16,16,896]{2,1,0:T(8,128)(2,1)S(1)}, u32[]{:S(2)}, u32[]{:S(2)}) async-start(bf16[16,16,896]{2,1,0:T(8,128)(2,1)} %bitcast.6), calls=%async_computation.1 | async-start | bytes 917504 | tf_op jit(solution)/shard_map/all_to_all | solution.py:96
  239.8 2.8 %copy-start.1 = (bf16[2,128,6,128]{3,2,0,1:T(8,128)(2,1)}, bf16[2,128,6,128]{3,2,0,1:T(8,128)(2,1)S(1)}, u32[]{:S(2)}) copy-start(bf16[2,128,6,128]{3,2,0,1:T(8,128)(2,1)S(1)} %copy.83) | copy-start | bytes 1179652
  243.1 5.5 %copy-start.2 = (bf16[128,64,256]{2,1,0:T(8,128)(2,1)S(1)}, bf16[128,64,256]{2,1,0:T(8,128)(2,1)}, u32[]{:S(2)}) copy-start(bf16[128,64,256]{2,1,0:T(8,128)(2,1)} %param.13) | copy-start | bytes 12582916
  246.4 2.9 %slice-start = ((bf16[2,128,256]{2,1,0:T(8,128)(2,1)}), bf16[2,128,128]{2,1,0:T(8,128)(2,1)S(1)}, s32[]{:S(2)}) async-start(bf16[2,128,256]{2,1,0:T(8,128)(2,1)} %param.12), calls=%async_computation.4 | async-start | bytes 131072 | tf_op jit(solution)/shard_map/slice | solution.py:110
where the time goes:
time: 254 us; the launch traced here: 251 us
  waiting for transfers between devices  193 us (76%)
  matrix products  25.5 us (10%)
  starting transfers between devices  22.2 us (9%)
  other arithmetic  7.72 us (3%)
  local copies, waits for them, and re-layouts  2.78 us (1%)
    all_to_all x2, waiting for transfers between devices, local(): lax.all_to_all(outgoing, 'rows', split_axis=0, concat_axis=0, tiled=True)  174 us
    all_to_all x2, waiting for transfers between devices, local(): lax.all_to_all(joined_delta.reshape(received.shape[0], received.shape[1],...  18.2 us
    all_to_all x2, starting transfers between devices, local(): lax.all_to_all(outgoing, 'rows', split_axis=0, concat_axis=0, tiled=True)  11.7 us
    all_to_all x2, starting transfers between devices, local(): lax.all_to_all(joined_delta.reshape(received.shape[0], received.shape[1],...  10.5 us
    dot_general x2, matrix products, local(): jnp.einsum('bc,bd->cd', placing, hidden[step_index], preferred_element_ty...  9.81 us
    dot_general x2, matrix products, local(): jnp.dot(flattened, down_projected, preferred_element_type=jnp.float32)  7.45 us
  transfers between devices with their start and end apart: 4, of which 4 were waited for; matrix products, arithmetic and copies ran while one was open for 6% of the time, Pallas kernels for 0%

commit v1 on v0

--- a/solution.py
+++ b/solution.py
@@ -1,8 +1,11 @@
+import functools
 import math
 
 import jax
 import jax.numpy as jnp
 from jax import lax
+from jax.experimental import pallas as pl
+from jax.experimental.pallas import tpu as pltpu
 from jax.sharding import PartitionSpec as P
 
 NEG = -1e30
@@ -41,6 +44,239 @@
         "sbgt,tbh->sbgh", weights[..., positions_n:], new_value, preferred_element_type=jnp.float32
     )
     return result.reshape(steps_n, block_rows, width_q).astype(jnp.bfloat16)
+
+
+def flipped(index, mask, bits):
+    result = 0
+    for bit in range(bits):
+        value = (index // (1 << bit)) % 2
+        if (mask >> bit) & 1:
+            value = 1 - value
+        result = result + value * (1 << bit)
+    return result
+
+
+def low_rank_kernel(
+    bits,
+    hidden_ref,
+    bank_ref,
+    slot_ref,
+    out_ref,
+    x_ref,
+    w_ref,
+    s_ref,
+    total_ref,
+    part_ref,
+    back_ref,
+    local_sem,
+    hidden_send,
+    hidden_recv,
+    slot_send,
+    slot_recv,
+    bank_send,
+    bank_recv,
+    part_send,
+    part_recv,
+):
+    peers = 1 << bits
+    half = peers // 2
+    steps_n, rows_here, width = hidden_ref.shape
+    chunk = width // half
+    rank2 = bank_ref.shape[2]
+    me = lax.axis_index("rows")
+    mine = me % half
+
+    def hidden_source(index):
+        return hidden_ref.at[:, :, pl.ds(pl.multiple_of(index * chunk, chunk), chunk)]
+
+    def bank_source(index):
+        return bank_ref.at[0, pl.ds(pl.multiple_of(index * chunk, chunk), chunk), :]
+
+    own_hidden = pltpu.make_async_copy(hidden_source(mine), x_ref.at[0], local_sem.at[0])
+    own_bank = pltpu.make_async_copy(
+        bank_source(mine), w_ref.at[:, pl.ds(0, rank2)], local_sem.at[1]
+    )
+    own_hidden.start()
+    own_bank.start()
+    s_ref[0] = slot_ref[...]
+
+    barrier = pltpu.get_barrier_semaphore()
+    for mask in range(1, peers):
+        pl.semaphore_signal(
+            barrier,
+            inc=1,
+            device_id={"rows": flipped(me, mask, bits)},
+            device_id_type=pl.DeviceIdType.MESH,
+        )
+    pl.semaphore_wait(barrier, peers - 1)
+
+    def remote(source, target, send, recv, mask):
+        return pltpu.make_async_remote_copy(
+            src_ref=source,
+            dst_ref=target,
+            send_sem=send.at[mask],
+            recv_sem=recv.at[mask],
+            device_id={"rows": flipped(me, mask, bits)},
+            device_id_type=pl.DeviceIdType.MESH,
+        )
+
+    sends = []
+    hidden_copies = {}
+    slot_copies = {}
+    bank_copies = {}
+    part_copies = {}
+    for mask in range(half - 1, 0, -1):
+        hidden_copies[mask] = remote(
+            hidden_source(flipped(mine, mask, bits - 1)),
+            x_ref.at[mask],
+            hidden_send,
+            hidden_recv,
+            mask,
+        )
+        slot_copies[mask] = remote(slot_ref, s_ref.at[mask], slot_send, slot_recv, mask)
+        hidden_copies[mask].start()
+        slot_copies[mask].start()
+        sends += [hidden_copies[mask], slot_copies[mask]]
+    for mask in range(1, peers):
+        bank_copies[mask] = remote(
+            bank_source(flipped(mine, mask % half, bits - 1)),
+            w_ref.at[:, pl.ds(mask * rank2, rank2)],
+            bank_send,
+            bank_recv,
+            mask,
+        )
+        bank_copies[mask].start()
+        sends.append(bank_copies[mask])
+
+    total_ref[...] = jnp.zeros_like(total_ref)
+    own_hidden.wait()
+    own_bank.wait()
+    for mask in range(1, half):
+        hidden_copies[mask].wait_recv()
+        slot_copies[mask].wait_recv()
+    for first in range(0, peers, 2):
+        for mask in (first, first + 1):
+            if mask:
+                bank_copies[mask].wait_recv()
+        owner_a = flipped(me, first, bits)
+        owner_b = flipped(me, first + 1, bits)
+
+        def multiply(source, carry, first=first, owner_a=owner_a, owner_b=owner_b):
+            rows = x_ref[source].reshape(steps_n * rows_here, chunk)
+            product = jnp.dot(
+                rows,
+                w_ref[:, first * rank2 : (first + 2) * rank2],
+                preferred_element_type=jnp.float32,
+            ).reshape(steps_n, rows_here, 2 * rank2)
+            slots = s_ref[source][None]
+            total_ref[source] = jnp.where(
+                slots == owner_a,
+                product[..., :rank2],
+                jnp.where(slots == owner_b, product[..., rank2:], total_ref[source]),
+            )
+            return carry
+
+        lax.fori_loop(0, half, multiply, 0)
+
+    part_ref[...] = total_ref[...].astype(jnp.bfloat16)
+    for mask in range(1, half):
+        part_copies[mask] = remote(
+            part_ref.at[mask], back_ref.at[mask], part_send, part_recv, mask
+        )
+        part_copies[mask].start()
+        sends.append(part_copies[mask])
+    result = total_ref[0]
+    for mask in range(1, half):
+        part_copies[mask].wait_recv()
+        result = result + back_ref[mask].astype(jnp.float32)
+    out_ref[...] = result.astype(jnp.bfloat16)
+    for copy in sends:
+        copy.wait_send()
+
+
+def low_rank_call(hidden, bank_down, slots, peers):
+    bits = peers.bit_length() - 1
+    half = peers // 2
+    steps_n, rows_here, width = hidden.shape
+    chunk = width // half
+    rank2 = bank_down.shape[2]
+    dma = pltpu.SemaphoreType.DMA
+    return pl.pallas_call(
+        functools.partial(low_rank_kernel, bits),
+        out_shape=jax.ShapeDtypeStruct((steps_n, rows_here, rank2), jnp.bfloat16),
+        in_specs=[
+            pl.BlockSpec(memory_space=pl.ANY),
+            pl.BlockSpec(memory_space=pl.ANY),
+            pl.BlockSpec(memory_space=pltpu.VMEM),
+        ],
+        out_specs=pl.BlockSpec(memory_space=pltpu.VMEM),
+        scratch_shapes=[
+            pltpu.VMEM((half, steps_n, rows_here, chunk), jnp.bfloat16),
+            pltpu.VMEM((chunk, peers * rank2), jnp.bfloat16),
+            pltpu.VMEM((half, rows_here, rank2), jnp.int32),
+            pltpu.VMEM((half, steps_n, rows_here, rank2), jnp.float32),
+            pltpu.VMEM((half, steps_n, rows_here, rank2), jnp.bfloat16),
+            pltpu.VMEM((half, steps_n, rows_here, rank2), jnp.bfloat16),
+            dma((2,)),
+            dma((half,)),
+            dma((half,)),
+            dma((half,)),
+            dma((half,)),
+            dma((peers,)),
+            dma((peers,)),
+            dma((half,)),
+            dma((half,)),
+        ],
+        compiler_params=pltpu.CompilerParams(
+            collective_id=0, has_side_effects=True, vmem_limit_bytes=40 * 1024 * 1024
+        ),
+        cost_estimate=pl.CostEstimate(
+            flops=2 * half * steps_n * rows_here * chunk * peers * rank2,
+            bytes_accessed=16 * 1024 * 1024,
+            transcendentals=0,
+        ),
+    )(hidden, bank_down, slots)
+
+
+def split_width(
+    hidden,
+    q_base,
+    kv_base,
+    cache,
+    lengths,
+    tenant,
+    slot_of_tenant,
+    bank_down,
+    adapter_query_up_stack,
+    adapter_key_up_stack,
+):
+    peers = lax.axis_size("rows")
+    steps_n, rows_here, _ = hidden.shape
+    head_dim = cache.shape[2] // 2
+    width_q = q_base.shape[2]
+    rank = adapter_query_up_stack.shape[1]
+    tenant_ids = jnp.arange(slot_of_tenant.shape[0], dtype=jnp.int32)
+    owner = jnp.sum(
+        jnp.where(tenant[:, None] == tenant_ids[None, :], slot_of_tenant[None, :], 0), axis=1
+    )
+    ups = jnp.concatenate([adapter_query_up_stack[0], adapter_key_up_stack[0]], axis=1)
+    ups = lax.all_gather(ups, "rows", axis=0, tiled=True)
+    slots = jnp.broadcast_to(owner[:, None], (rows_here, 2 * rank)).astype(jnp.int32)
+    low_rank = low_rank_call(hidden, bank_down, slots, peers)
+    chosen = owner[:, None] == jnp.arange(peers, dtype=jnp.int32)[None, :]
+
+    def correction(part, up):
+        placed = jnp.where(chosen[None, :, :, None], part[:, :, None, :], 0)
+        placed = placed.reshape(steps_n * rows_here, peers * rank).astype(jnp.bfloat16)
+        product = jnp.dot(placed, up, preferred_element_type=jnp.float32).astype(jnp.bfloat16)
+        return product.astype(jnp.float32).reshape(steps_n, rows_here, up.shape[1])
+
+    delta_q = correction(low_rank[..., :rank], ups[:, :width_q])
+    delta_k = correction(low_rank[..., rank:], ups[:, width_q:])
+    query = (q_base.astype(jnp.float32) + delta_q).astype(jnp.bfloat16)
+    new_key = (kv_base[..., :head_dim].astype(jnp.float32) + delta_k).astype(jnp.bfloat16)
+    new_value = kv_base[..., head_dim:]
+    return attend(query, new_key, new_value, cache[..., :head_dim], cache[..., head_dim:], lengths)
 
 
 def local(
@@ -112,8 +348,10 @@
 
 
 def solution(mesh):
+    peers = mesh.shape["rows"]
+    small = 4 <= peers <= 16 and peers & (peers - 1) == 0
     return jax.shard_map(
-        local,
+        split_width if small else local,
         mesh=mesh,
         in_specs=(
             P(None, ("groups", "rows"), None),

time: 254 us -> 184 us (0.72); the launches traced: 251 us -> 184 us
  waiting for transfers between devices: 193 us -> 0.04 us
  Pallas kernels: 0 us -> 147 us
  starting transfers between devices: 22.2 us -> 0.01 us
  matrix products: 25.5 us -> 9.76 us
  between operations: 0.25 us -> 13.6 us
  local copies, waits for them, and re-layouts: 2.78 us -> 7.27 us
    all_to_all x4 -> x0, waiting for transfers between devices: 193 us -> none  [the longest x2 174 us: local(): lax.all_to_all(outgoing, 'rows', split_axis=0, concat_axis=0, tiled=True)]
    pallas_call x0 -> x1, Pallas kernels: none -> 147 us  [low_rank_call(): pl.pallas_call(functools.partial(low_rank_kernel, bits), out_shape=jax.Sh...]
    all_to_all x4 -> x0, starting transfers between devices: 22.2 us -> none  [the longest x2 11.7 us: local(): lax.all_to_all(outgoing, 'rows', split_axis=0, concat_axis=0, tiled=True)]
    dot_general x10 -> x2, matrix products: 18.7 us -> 3.31 us  [correction(): jnp.dot(placed, up, preferred_element_type=jnp.float32).astype(jnp.bfloat16)]
    unnamed x12 -> x13, local copies, waits for them, and re-layouts: 0.03 us -> 4.09 us
  transfers between devices with their start and end apart: 4 -> 1, of which waited for: 4 -> 0; matrix products, arithmetic and copies ran while one was open for 6% -> 1% of each run, Pallas kernels for 0% -> 80%
where the time goes in v1:
time: 184 us
  Pallas kernels  147 us (80%)
  between operations  13.6 us (7%)
  matrix products  9.76 us (5%)
  local copies, waits for them, and re-layouts  7.27 us (4%)
  other arithmetic  5.65 us (3%)
    pallas_call x1, Pallas kernels, low_rank_call(): pl.pallas_call(functools.partial(low_rank_kernel, bits), out_shape=jax.Sh...  147 us
    unnamed x13, local copies, waits for them, and re-layouts  4.09 us
  transfers between devices with their start and end apart: 1, of which 0 were waited for; matrix products, arithmetic and copies ran while one was open for 1% of the time, Pallas kernels for 80%

profile of v1, /device:TPU:17, one launch (start us, length us, event | category | flops | bytes accessed | tf_op | source)
XLA Modules:
  0.0 183.7 jit_solution(10530040760602899253)
XLA Ops:
  6.5 1.6 pad_maximum_fusion
  8.1 0.8 select_reduce_fusion
  9.0 2.2 %copy-done = bf16[2,128,8192]{2,1,0:T(8,128)(2,1)S(1)} copy-done((bf16[2,128,8192]{2,1,0:T(8,128)(2,1)S(1)}, bf16[2,128,8192]{2,1,0:T(8,128)(2,1)}, u32[]{:S(2)}) %copy-start) | copy-done | bytes 4194328
  11.2 1.6 copy-done.1
  12.8 147.3 %shard_map.100 = bf16[2,128,128]{2,1,0:T(8,128)(2,1)S(1)} custom-call(bf16[2,128,8192]{2,1,0:T(8,128)(2,1)S(1)} %copy-done, bf16[1,8192,128]{2,1,0:T(8,128)(2,1)S(1)} %copy-done.1, s32[128,128]{1,0:T(8,128)S(1)} %broadcast_in_dim.92.slot_ref), custom_call_target="tpu_custom_call" | custom-call | flops 8589934592 | bytes 16777216 | tf_op jit(solution)/shard_map/pallas_call | solution.py:204
  160.4 0.2 copy.83
  160.8 0.8 broadcast_select_fusion
  161.7 1.3 convolution_convert_fusion
  163.0 2.0 %fusion.18 = bf16[256,768]{1,0:T(8,128)(2,1)S(1)} fusion(bf16[1024,896]{1,0:T(8,128)(2,1)} %all-gather.2.cloned.1.call-done, bf16[128,8,2,128]{3,2,1,0:T(2,128)(2,1)S(1)} %bitcast.58), kind=kOutput, calls=%fused_computation.13 | convolution fusion | flops 402849792 | bytes 2490368 | tf_op jit(solution)/shard_map/dot_general | solution.py:271
  165.0 0.2 copy.85
  165.3 0.4 copy.86
  165.7 2.4 %fusion.33 = f32[128,2,2,6]{3,1,2,0:T(2,128)S(1)} fusion(bf16[2,128,6,128]{3,2,0,1:T(8,128)(2,1)S(1)} %copy.86, bf16[2,128,128,1]{2,1,0,3:T(8,128)(2,1)S(1)} %fusion.32), kind=kOutput, calls=%fused_computation.35 | convolution fusion | flops 786432 | bytes 471040 | tf_op jit(solution)/shard_map/sbgh,tbh->sbgt/dot_general | solution.py:28
  168.1 0.1 copy.90
  168.2 0.1 fusion.35
  168.3 0.2 copy.92
  168.5 0.5 copy.91
  169.0 3.0 %fusion.37 = (f32[2,128,6]{2,0,1:T(2,128)S(1)}, f32[2,128,6,64]{3,2,0,1:T(8,128)S(1)}) fusion(bf16[2,128,6,128]{3,2,0,1:T(8,128)(2,1)S(1)} %copy.86, bf16[128,64,256]{2,1,0:T(8,128)(2,1)} %param.13, pred[128,64]{1,0:T(8,128)(4,1)S(1)} %iota_compare_fusion), kind=kOutput, calls=%fused_computation.45 | convolution fusion | flops 25459200 | bytes 2897920 | tf_op jit(solution)/shard_map/sbgh,bch->sbgc/dot_general | solution.py:22
  172.1 1.1 fusion.30
  173.2 1.0 divide_convert_fusion
  174.3 0.7 fusion
  175.0 0.1 slice-done
  175.1 0.4 fusion.21
  175.5 0.4 copy.95
  175.9 0.9 copy.96
  (24 shorter events, 0.8 us)
Async XLA Ops:
  6.5 155.1 %all-gather.2.cloned.1.call-start = ((), (), s32[]{:S(2)}) async-start(), calls=%async_computation | async-start | bytes 1949696 | tf_op jit(solution)/shard_map/all_gather | solution.py:263
  9.0 2.2 %copy-start = (bf16[2,128,8192]{2,1,0:T(8,128)(2,1)S(1)}, bf16[2,128,8192]{2,1,0:T(8,128)(2,1)}, u32[]{:S(2)}) copy-start(bf16[2,128,8192]{2,1,0:T(8,128)(2,1)} %hidden_ref.1) | copy-start | bytes 12582916
  11.2 1.6 copy-start.1
  12.8 147.7 %copy-start.3 = (bf16[2,128,768]{2,1,0:T(8,128)(2,1)S(1)}, bf16[2,128,768]{2,1,0:T(8,128)(2,1)}, u32[]{:S(2)}) copy-start(bf16[2,128,768]{2,1,0:T(8,128)(2,1)} %param.11) | copy-start | bytes 1179652
  12.8 147.9 %copy-start.5 = (s32[128]{0:T(128)S(1)}, s32[128]{0:T(128)}, u32[]{:S(2)}) copy-start(s32[128]{0:T(128)} %param.14) | copy-start | bytes 1540
  160.1 2.9 %copy-start.4 = (bf16[2,128,256]{2,1,0:T(8,128)(2,1)S(1)}, bf16[2,128,256]{2,1,0:T(8,128)(2,1)}, u32[]{:S(2)}) copy-start(bf16[2,128,256]{2,1,0:T(8,128)(2,1)} %param.12) | copy-start | bytes 393220
  172.1 2.2 %copy-start.2 = (bf16[128,64,256]{2,1,0:T(8,128)(2,1)S(1)}, bf16[128,64,256]{2,1,0:T(8,128)(2,1)}, u32[]{:S(2)}) copy-start(bf16[128,64,256]{2,1,0:T(8,128)(2,1)} %param.13) | copy-start | bytes 12582916
  174.3 0.8 slice-start
Sparse Core Ops, SparseCore 0:
  9.6 79.0 all-gather.1

commit v2 on v1

--- a/solution.py
+++ b/solution.py
@@ -65,6 +65,7 @@
     x_ref,
     w_ref,
     s_ref,
+    column_ref,
     total_ref,
     part_ref,
     back_ref,
@@ -85,6 +86,7 @@
     rank2 = bank_ref.shape[2]
     me = lax.axis_index("rows")
     mine = me % half
+    group = 2
 
     def hidden_source(index):
         return hidden_ref.at[:, :, pl.ds(pl.multiple_of(index * chunk, chunk), chunk)]
@@ -94,7 +96,7 @@
 
     own_hidden = pltpu.make_async_copy(hidden_source(mine), x_ref.at[0], local_sem.at[0])
     own_bank = pltpu.make_async_copy(
-        bank_source(mine), w_ref.at[:, pl.ds(0, rank2)], local_sem.at[1]
+        bank_source(mine), w_ref.at[0], local_sem.at[1]
     )
     own_hidden.start()
     own_bank.start()
@@ -120,12 +122,11 @@
             device_id_type=pl.DeviceIdType.MESH,
         )
 
-    sends = []
     hidden_copies = {}
     slot_copies = {}
     bank_copies = {}
     part_copies = {}
-    for mask in range(half - 1, 0, -1):
+    for mask in range(1, half):
         hidden_copies[mask] = remote(
             hidden_source(flipped(mine, mask, bits - 1)),
             x_ref.at[mask],
@@ -134,26 +135,28 @@
             mask,
         )
         slot_copies[mask] = remote(slot_ref, s_ref.at[mask], slot_send, slot_recv, mask)
-        hidden_copies[mask].start()
-        slot_copies[mask].start()
-        sends += [hidden_copies[mask], slot_copies[mask]]
     for mask in range(1, peers):
         bank_copies[mask] = remote(
             bank_source(flipped(mine, mask % half, bits - 1)),
-            w_ref.at[:, pl.ds(mask * rank2, rank2)],
+            w_ref.at[mask],
             bank_send,
             bank_recv,
             mask,
         )
+    sends = [*hidden_copies.values(), *slot_copies.values(), *bank_copies.values()]
+    for mask in range(half - 1, 0, -1):
+        hidden_copies[mask].start()
+        slot_copies[mask].start()
+    for mask in range(1, peers):
         bank_copies[mask].start()
-        sends.append(bank_copies[mask])
-
     total_ref[...] = jnp.zeros_like(total_ref)
     own_hidden.wait()
     own_bank.wait()
     for mask in range(1, half):
         hidden_copies[mask].wait_recv()
         slot_copies[mask].wait_recv()
+    for mask in range(half):
+        column_ref[mask] = jnp.broadcast_to(s_ref[mask][:1], (rank2, rows_here)).T
     for first in range(0, peers, 2):
         for mask in (first, first + 1):
             if mask:
@@ -162,29 +165,34 @@
         owner_b = flipped(me, first + 1, bits)
 
         def multiply(source, carry, first=first, owner_a=owner_a, owner_b=owner_b):
-            rows = x_ref[source].reshape(steps_n * rows_here, chunk)
+            some = pl.ds(source * group, group)
             product = jnp.dot(
-                rows,
-                w_ref[:, first * rank2 : (first + 2) * rank2],
+                x_ref[some].reshape(group * steps_n * rows_here, chunk),
+                jnp.concatenate([w_ref[first], w_ref[first + 1]], axis=1),
                 preferred_element_type=jnp.float32,
-            ).reshape(steps_n, rows_here, 2 * rank2)
-            slots = s_ref[source][None]
-            total_ref[source] = jnp.where(
+            ).reshape(group, steps_n, rows_here, 2 * rank2)
+            slots = column_ref[some][:, None]
+            total_ref[some] = jnp.where(
                 slots == owner_a,
                 product[..., :rank2],
-                jnp.where(slots == owner_b, product[..., rank2:], total_ref[source]),
+                jnp.where(slots == owner_b, product[..., rank2:], total_ref[some]),
             )
             return carry
 
-        lax.fori_loop(0, half, multiply, 0)
-
-    part_ref[...] = total_ref[...].astype(jnp.bfloat16)
-    for mask in range(1, half):
-        part_copies[mask] = remote(
-            part_ref.at[mask], back_ref.at[mask], part_send, part_recv, mask
-        )
-        part_copies[mask].start()
-        sends.append(part_copies[mask])
+        if first != peers - 2:
+            lax.fori_loop(0, half // group, multiply, 0)
+            continue
+        for block in reversed(range(half // group)):
+            multiply(block, 0)
+            for mask in range(block * group, (block + 1) * group):
+                if mask:
+                    part_ref[mask] = total_ref[mask].astype(jnp.bfloat16)
+                    part_copies[mask] = remote(
+                        part_ref.at[mask], back_ref.at[mask], part_send, part_recv, mask
+                    )
+                    part_copies[mask].start()
+                    sends.append(part_copies[mask])
+
     result = total_ref[0]
     for mask in range(1, half):
         part_copies[mask].wait_recv()
@@ -212,7 +220,8 @@
         out_specs=pl.BlockSpec(memory_space=pltpu.VMEM),
         scratch_shapes=[
             pltpu.VMEM((half, steps_n, rows_here, chunk), jnp.bfloat16),
-            pltpu.VMEM((chunk, peers * rank2), jnp.bfloat16),
+            pltpu.VMEM((peers, chunk, rank2), jnp.bfloat16),
+            pltpu.VMEM((half, *slots.shape), jnp.int32),
             pltpu.VMEM((half, rows_here, rank2), jnp.int32),
             pltpu.VMEM((half, steps_n, rows_here, rank2), jnp.float32),
             pltpu.VMEM((half, steps_n, rows_here, rank2), jnp.bfloat16),
@@ -228,7 +237,7 @@
             dma((half,)),
         ],
         compiler_params=pltpu.CompilerParams(
-            collective_id=0, has_side_effects=True, vmem_limit_bytes=40 * 1024 * 1024
+            collective_id=0, has_side_effects=True, vmem_limit_bytes=60 * 1024 * 1024
         ),
         cost_estimate=pl.CostEstimate(
             flops=2 * half * steps_n * rows_here * chunk * peers * rank2,
@@ -261,7 +270,7 @@
     )
     ups = jnp.concatenate([adapter_query_up_stack[0], adapter_key_up_stack[0]], axis=1)
     ups = lax.all_gather(ups, "rows", axis=0, tiled=True)
-    slots = jnp.broadcast_to(owner[:, None], (rows_here, 2 * rank)).astype(jnp.int32)
+    slots = jnp.broadcast_to(owner[None, :], (8, rows_here)).astype(jnp.int32)
     low_rank = low_rank_call(hidden, bank_down, slots, peers)
     chosen = owner[:, None] == jnp.arange(peers, dtype=jnp.int32)[None, :]
 

time: 184 us -> 175 us (0.951)
  Pallas kernels: 147 us -> 141 us
  local copies, waits for them, and re-layouts: 7.27 us -> 4.91 us
    pallas_call x1, Pallas kernels: 147 us -> 141 us  [low_rank_call(): pl.pallas_call(functools.partial(low_rank_kernel, bits), out_shape=jax.Sh...]
    unnamed x13 -> x9, local copies, waits for them, and re-layouts: 4.09 us -> 0.3 us
  transfers between devices with their start and end apart: 1 -> 1, of which waited for: 0 -> 0; matrix products, arithmetic and copies ran while one was open for 1% -> 2% of each run, Pallas kernels for 80% -> 81%
where the time goes in v2:
time: 175 us
  Pallas kernels  141 us (81%)
  between operations  13.6 us (8%)
  matrix products  9.75 us (6%)
  other arithmetic  5.65 us (3%)
  local copies, waits for them, and re-layouts  4.91 us (3%)
    pallas_call x1, Pallas kernels, low_rank_call(): pl.pallas_call(functools.partial(low_rank_kernel, bits), out_shape=jax.Sh...  141 us
  transfers between devices with their start and end apart: 1, of which 0 were waited for; matrix products, arithmetic and copies ran while one was open for 2% of the time, Pallas kernels for 81%

profile of v2, /device:TPU:17, one launch (start us, length us, event | category | flops | bytes accessed | tf_op | source)
XLA Modules:
  0.0 174.6 jit_solution(7423110101663379619)
XLA Ops:
  6.5 1.6 pad_maximum_fusion
  8.1 0.8 select_reduce_fusion
  8.9 0.6 broadcast_in_dim.92.slot_ref
  9.5 140.6 %shard_map.100 = bf16[2,128,128]{2,1,0:T(8,128)(2,1)} custom-call(bf16[2,128,8192]{2,1,0:T(8,128)(2,1)} %hidden_ref.1, bf16[1,8192,128]{2,1,0:T(8,128)(2,1)} %bank_ref.1, s32[8,128]{1,0:T(8,128)} %broadcast_in_dim.92.slot_ref), custom_call_target="tpu_custom_call" | custom-call | flops 8589934592 | bytes 16777216 | tf_op jit(solution)/shard_map/pallas_call | solution.py:212
  150.1 1.0 fusion.36
  151.3 0.2 copy.83
  151.7 0.8 broadcast_select_fusion
  152.6 1.3 convolution_convert_fusion
  153.9 2.0 %fusion.18 = bf16[256,768]{1,0:T(8,128)(2,1)S(1)} fusion(bf16[1024,896]{1,0:T(8,128)(2,1)} %all-gather.2.cloned.1.call-done, bf16[128,8,2,128]{3,2,1,0:T(2,128)(2,1)S(1)} %bitcast.58), kind=kOutput, calls=%fused_computation.13 | convolution fusion | flops 402849792 | bytes 2490368 | tf_op jit(solution)/shard_map/dot_general | solution.py:280
  155.9 0.2 copy.85
  156.2 0.4 copy.86
  156.6 2.4 %fusion.33 = f32[128,2,2,6]{3,1,2,0:T(2,128)S(1)} fusion(bf16[2,128,6,128]{3,2,0,1:T(8,128)(2,1)S(1)} %copy.86, bf16[2,128,128,1]{2,1,0,3:T(8,128)(2,1)S(1)} %fusion.32), kind=kOutput, calls=%fused_computation.35 | convolution fusion | flops 786432 | bytes 471040 | tf_op jit(solution)/shard_map/sbgh,tbh->sbgt/dot_general | solution.py:28
  159.0 0.1 copy.90
  159.1 0.1 fusion.35
  159.3 0.2 copy.92
  159.4 0.5 copy.91
  159.9 3.0 %fusion.37 = (f32[2,128,6]{2,0,1:T(2,128)S(1)}, f32[2,128,6,64]{3,2,0,1:T(8,128)S(1)}) fusion(bf16[2,128,6,128]{3,2,0,1:T(8,128)(2,1)S(1)} %copy.86, bf16[128,64,256]{2,1,0:T(8,128)(2,1)} %param.13, pred[128,64]{1,0:T(8,128)(4,1)S(1)} %iota_compare_fusion), kind=kOutput, calls=%fused_computation.45 | convolution fusion | flops 25459200 | bytes 2897920 | tf_op jit(solution)/shard_map/sbgh,bch->sbgc/dot_general | solution.py:22
  163.0 1.1 fusion.30
  164.1 1.0 divide_convert_fusion
  165.2 0.7 fusion
  165.9 0.1 slice-done
  166.0 0.4 fusion.21
  166.4 0.4 copy.95
  166.8 0.9 copy.96
  (20 shorter events, 0.6 us)
Async XLA Ops:
  6.5 146.0 %all-gather.2.cloned.1.call-start = ((), (), s32[]{:S(2)}) async-start(), calls=%async_computation | async-start | bytes 1949696 | tf_op jit(solution)/shard_map/all_gather | solution.py:272
  9.5 141.9 %copy-start.1 = (bf16[2,128,768]{2,1,0:T(8,128)(2,1)S(1)}, bf16[2,128,768]{2,1,0:T(8,128)(2,1)}, u32[]{:S(2)}) copy-start(bf16[2,128,768]{2,1,0:T(8,128)(2,1)} %param.11) | copy-start | bytes 1179652
  9.5 142.1 %copy-start.3 = (s32[128]{0:T(128)S(1)}, s32[128]{0:T(128)}, u32[]{:S(2)}) copy-start(s32[128]{0:T(128)} %param.14) | copy-start | bytes 1540
  150.1 3.8 %copy-start.2 = (bf16[2,128,256]{2,1,0:T(8,128)(2,1)S(1)}, bf16[2,128,256]{2,1,0:T(8,128)(2,1)}, u32[]{:S(2)}) copy-start(bf16[2,128,256]{2,1,0:T(8,128)(2,1)} %param.12) | copy-start | bytes 393220
  163.0 2.2 %copy-start = (bf16[128,64,256]{2,1,0:T(8,128)(2,1)S(1)}, bf16[128,64,256]{2,1,0:T(8,128)(2,1)}, u32[]{:S(2)}) copy-start(bf16[128,64,256]{2,1,0:T(8,128)(2,1)} %param.13) | copy-start | bytes 12582916
  165.2 0.8 slice-start
Sparse Core Ops, SparseCore 0:
  9.6 73.8 all-gather.1

commit v3 on v2

--- a/solution.py
+++ b/solution.py
@@ -24,8 +24,15 @@
     )
     in_cache = jnp.arange(positions_n, dtype=jnp.int32)[None, :] < length_block[:, None]
     scores = jnp.where(in_cache[None, :, None, :], scores, NEG)
+    wide_heads = query_heads.astype(jnp.float32)
     own_scores = (
-        jnp.einsum("sbgh,tbh->sbgt", query_heads, new_key, preferred_element_type=jnp.float32)
+        jnp.stack(
+            [
+                jnp.sum(wide_heads * new_key[t].astype(jnp.float32)[None, :, None, :], axis=-1)
+                for t in range(steps_n)
+            ],
+            axis=-1,
+        )
         * score_scale
     )
     causal = jnp.arange(steps_n)[None, :] <= jnp.arange(steps_n)[:, None]

time: 175 us -> 173 us (0.989)
  matrix products: 9.75 us -> 7.37 us
    dot_general x1 -> x0, matrix products: 2.39 us -> none  [attend(): jnp.einsum('sbgh,tbh->sbgt', query_heads, new_key, preferred_element_type...]
  transfers between devices with their start and end apart: 1 -> 1, of which waited for: 0 -> 0; matrix products, arithmetic and copies ran while one was open for 2% -> 2% of each run, Pallas kernels for 81% -> 82%
where the time goes in v3:
time: 173 us; the launch traced here: 172 us
  Pallas kernels  141 us (82%)
  between operations  13.6 us (8%)
  matrix products  7.37 us (4%)
  other arithmetic  5.8 us (3%)
  local copies, waits for them, and re-layouts  5 us (3%)
    pallas_call x1, Pallas kernels, low_rank_call(): pl.pallas_call(functools.partial(low_rank_kernel, bits), out_shape=jax.Sh...  141 us
  transfers between devices with their start and end apart: 1, of which 0 were waited for; matrix products, arithmetic and copies ran while one was open for 2% of the time, Pallas kernels for 82%

profile of v3, /device:TPU:17, one launch (start us, length us, event | category | flops | bytes accessed | tf_op | source)
XLA Modules:
  0.0 172.5 jit_solution(4157191844323011061)
XLA Ops:
  6.5 1.6 pad_maximum_fusion
  8.1 0.8 select_reduce_fusion
  8.9 0.6 broadcast_in_dim.94.slot_ref
  9.5 140.6 %shard_map.100 = bf16[2,128,128]{2,1,0:T(8,128)(2,1)} custom-call(bf16[2,128,8192]{2,1,0:T(8,128)(2,1)} %hidden_ref.1, bf16[1,8192,128]{2,1,0:T(8,128)(2,1)} %bank_ref.1, s32[8,128]{1,0:T(8,128)} %broadcast_in_dim.94.slot_ref), custom_call_target="tpu_custom_call" | custom-call | flops 8589934592 | bytes 16777216 | tf_op jit(solution)/shard_map/pallas_call | solution.py:219
  150.1 1.0 fusion.39
  151.2 0.1 copy.107
  151.3 0.1 copy.104
  151.4 0.2 copy.103
  151.7 0.8 broadcast_select_fusion
  152.6 1.3 convolution_convert_fusion
  154.2 2.0 %fusion.18 = bf16[256,768]{1,0:T(8,128)(2,1)S(1)} fusion(bf16[1024,896]{1,0:T(8,128)(2,1)} %all-gather.2.cloned.1.call-done, bf16[128,8,2,128]{3,2,1,0:T(2,128)(2,1)S(1)} %bitcast.65), kind=kOutput, calls=%fused_computation.13 | convolution fusion | flops 402849792 | bytes 2490368 | tf_op jit(solution)/shard_map/dot_general | solution.py:287
  156.2 0.2 copy.105
  156.4 0.4 copy.106
  156.9 0.2 fusion.23
  157.2 0.2 copy.115
  157.3 0.5 copy.114
  157.8 3.0 %fusion.40 = (f32[2,128,6]{2,0,1:T(2,128)S(1)}, f32[2,128,6,64]{3,2,0,1:T(8,128)S(1)}) fusion(bf16[2,128,6,128]{3,2,0,1:T(8,128)(2,1)S(1)} %copy.106, bf16[128,64,256]{2,1,0:T(8,128)(2,1)} %param.13, pred[128,64]{1,0:T(8,128)(4,1)S(1)} %iota_compare_fusion), kind=kOutput, calls=%fused_computation.51 | convolution fusion | flops 25459200 | bytes 2897920 | tf_op jit(solution)/shard_map/sbgh,bch->sbgc/dot_general | solution.py:22
  160.9 1.1 fusion.32
  162.0 1.0 divide_convert_fusion
  163.1 0.7 fusion
  163.8 0.1 slice-done
  163.9 0.4 fusion.21
  164.3 0.4 copy.118
  164.7 0.9 copy.119
  (24 shorter events, 0.7 us)
Async XLA Ops:
  6.5 146.1 %all-gather.2.cloned.1.call-start = ((), (), s32[]{:S(2)}) async-start(), calls=%async_computation | async-start | bytes 1949696 | tf_op jit(solution)/shard_map/all_gather | solution.py:279
  9.5 141.9 %copy-start.1 = (bf16[2,128,768]{2,1,0:T(8,128)(2,1)S(1)}, bf16[2,128,768]{2,1,0:T(8,128)(2,1)}, u32[]{:S(2)}) copy-start(bf16[2,128,768]{2,1,0:T(8,128)(2,1)} %param.11) | copy-start | bytes 1179652
  9.5 142.1 %copy-start.3 = (s32[128]{0:T(128)S(1)}, s32[128]{0:T(128)}, u32[]{:S(2)}) copy-start(s32[128]{0:T(128)} %param.14) | copy-start | bytes 1540
  150.1 3.8 %copy-start.2 = (bf16[2,128,256]{2,1,0:T(8,128)(2,1)S(1)}, bf16[2,128,256]{2,1,0:T(8,128)(2,1)}, u32[]{:S(2)}) copy-start(bf16[2,128,256]{2,1,0:T(8,128)(2,1)} %param.12) | copy-start | bytes 393220
  160.9 2.2 %copy-start = (bf16[128,64,256]{2,1,0:T(8,128)(2,1)S(1)}, bf16[128,64,256]{2,1,0:T(8,128)(2,1)}, u32[]{:S(2)}) copy-start(bf16[128,64,256]{2,1,0:T(8,128)(2,1)} %param.13) | copy-start | bytes 12582916
  163.1 0.8 slice-start
Sparse Core Ops, SparseCore 0:
  9.6 73.8 all-gather.1
